TPU v7x, 256 devices: a whole 4x4x8 slice. The times are simulated.
256 devices in a mesh: dp: 4 (over y), expert: 64 (over x, z, core).
Axes of the slice: x: 4, y: 4, z: 8, core: 2. Of those that a mesh axis runs over, the one named last changes fastest.
Arguments:
- tokens: bfloat16 [32768, 2048], P(('dp', 'expert')), may hold values from -6 to 6
- out_grad: bfloat16 [32768, 2048], P(('dp', 'expert')), may hold values from -6 to 6
- routes: int32 [32768, 4], P(('dp', 'expert')), may hold values from 0 to 63, all different within a row; in each aligned block of 128 rows (0 to 127, 128 to 255, ...) at most 9 rows name the same one
- gate_values: float32 [32768, 4], P(('dp', 'expert')), may hold values from 0.05 to 1
- w_gate: bfloat16 [64, 2048, 768], P('expert', 'dp'), may hold values from -0.125 to 0.125
- w_up: bfloat16 [64, 2048, 768], P('expert', 'dp'), may hold values from -0.125 to 0.125
- w_down: bfloat16 [64, 768, 2048], P('expert', None, 'dp'), may hold values from -0.21875 to 0.21875
Outputs:
- input_grad: bfloat16 [32768, 2048], P(('dp', 'expert'))
- gate_grad: bfloat16 [64, 2048, 768], P('expert', 'dp')
- up_grad: bfloat16 [64, 2048, 768], P('expert', 'dp')
- down_grad: bfloat16 [64, 768, 2048], P('expert', None, 'dp')
Inputs may be any that keep to these rules, and one draw needn't show every extreme that they name: `routes`: each token names 4 different experts. Among the 128 tokens of one device (aligned blocks of 128 tokens) no expert is named by more than 9 tokens, and in every draw some device names some expert exactly 9 times.
All inputs are finite; a program needn't handle non-finite values.
Results may differ from a plain program's by a relative error of at most 0.0095.
Values may be sent and summed in bfloat16 or wider, within the bound.
A program may use at most 128 MiB of HBM per device.

v0:
```python
import jax
import jax.numpy as jnp
from jax import lax
from jax.sharding import PartitionSpec as P


def local(tokens, out_grad, routes, gate_values, w_gate, w_up, w_down):
    tok_rows, model_width = tokens.shape
    top_count = routes.shape[1]
    group_count = lax.axis_size("expert")
    local_count = w_gate.shape[0]
    expert_count = group_count * local_count
    hidden_units = w_gate.shape[2]
    capacity = min(tok_rows, max(2, 9 * tok_rows * top_count // (8 * expert_count)))
    pair_count = tok_rows * top_count
    slot_count = group_count * capacity
    expert_of = routes.reshape(-1)
    onehot = (expert_of[:, None] == jnp.arange(expert_count, dtype=jnp.int32)[None, :]).astype(
        jnp.int32
    )
    before = jnp.cumsum(onehot, axis=0) - onehot
    placed = jnp.sum(before * onehot, axis=1)
    slot_of = expert_of * capacity + placed
    slot_table = jnp.full((expert_count * capacity,), pair_count, jnp.int32)
    slot_table = slot_table.at[slot_of].set(jnp.arange(pair_count, dtype=jnp.int32))
    filled = slot_table < pair_count
    source = jnp.where(filled, slot_table, 0)
    owner_row = source // top_count
    send_x = jnp.where(filled[:, None], tokens[owner_row], jnp.zeros((), jnp.bfloat16))
    scaled = gate_values.reshape(-1)[source][:, None] * out_grad[owner_row].astype(jnp.float32)
    send_dy = jnp.where(filled[:, None], scaled, 0.0).astype(jnp.bfloat16)
    send_x = send_x.reshape(expert_count, capacity, model_width)
    send_dy = send_dy.reshape(expert_count, capacity, model_width)
    recv_x, recv_dy = (
        lax.all_to_all(send_x, "expert", split_axis=0, concat_axis=0, tiled=True),
        lax.all_to_all(send_dy, "expert", split_axis=0, concat_axis=0, tiled=True),
    )

    def to_local(stacked):
        shaped = stacked.reshape(group_count, local_count, capacity, model_width)
        return shaped.transpose(1, 0, 2, 3).reshape(local_count, slot_count, model_width)

    slot_x = to_local(recv_x)
    slot_dy = to_local(recv_dy)
    part_x = slot_x
    gate_term = jnp.einsum(
        "asd,adf->asf",
        part_x,
        lax.all_gather(w_gate, "dp", axis=1, tiled=True),
        preferred_element_type=jnp.float32,
    )
    up_term = jnp.einsum(
        "asd,adf->asf",
        part_x,
        lax.all_gather(w_up, "dp", axis=1, tiled=True),
        preferred_element_type=jnp.float32,
    )
    full_gate, full_up, full_down = (
        lax.all_gather(w_gate, "dp", axis=1, tiled=True),
        lax.all_gather(w_up, "dp", axis=1, tiled=True),
        lax.all_gather(w_down, "dp", axis=2, tiled=True),
    )
    sigma = jax.nn.sigmoid(gate_term)
    active = gate_term * sigma
    activated = (active * up_term).astype(jnp.bfloat16)
    back_hidden = jnp.einsum("asd,afd->asf", slot_dy, full_down, preferred_element_type=jnp.float32)
    up_delta = (back_hidden * active).astype(jnp.bfloat16)
    gate_delta = (back_hidden * up_term * sigma * (1.0 + gate_term * (1.0 - sigma))).astype(
        jnp.bfloat16
    )
    pair_grad = (
        jnp.einsum("asf,adf->asd", gate_delta, full_gate, preferred_element_type=jnp.float32)
        + jnp.einsum("asf,adf->asd", up_delta, full_up, preferred_element_type=jnp.float32)
    ).astype(jnp.bfloat16)
    send_back = pair_grad.reshape(local_count, group_count, capacity, model_width).transpose(
        1, 0, 2, 3
    )
    send_back = send_back.reshape(expert_count, capacity, model_width)
    returned = lax.all_to_all(send_back, "expert", split_axis=0, concat_axis=0, tiled=True)
    per_pair = returned.reshape(expert_count * capacity, model_width)[slot_of].astype(jnp.float32)
    input_grad = jnp.sum(per_pair.reshape(tok_rows, top_count, model_width), axis=1).astype(
        jnp.bfloat16
    )
    block_width = local_count * hidden_units
    share_width = model_width // lax.axis_size("dp")
    part_x = slot_x
    term_gate = jnp.einsum("asd,asf->daf", part_x, gate_delta, preferred_element_type=jnp.float32)
    term_up = jnp.einsum("asd,asf->daf", part_x, up_delta, preferred_element_type=jnp.float32)
    term_down = jnp.einsum("asd,asf->daf", slot_dy, activated, preferred_element_type=jnp.float32)
    shares = lax.psum_scatter(
        jnp.concatenate(
            [
                term_gate.reshape(lax.axis_size("dp") * share_width, block_width),
                term_up.reshape(lax.axis_size("dp") * share_width, block_width),
                term_down.reshape(lax.axis_size("dp") * share_width, block_width),
            ],
            axis=1,
        ).astype(jnp.bfloat16),
        "dp",
        scatter_dimension=0,
        tiled=True,
    ).astype(jnp.float32)
    share_rows = shares.shape[0]

    def unpack(which):
        return shares[:, which * block_width : (which + 1) * block_width].reshape(
            share_rows, local_count, hidden_units
        )

    gate_grad = unpack(0).transpose(1, 0, 2).astype(jnp.bfloat16)
    up_grad = unpack(1).transpose(1, 0, 2).astype(jnp.bfloat16)
    down_grad = unpack(2).transpose(1, 2, 0).astype(jnp.bfloat16)
    return (input_grad, gate_grad, up_grad, down_grad)


def solution(mesh):
    return jax.shard_map(
        local,
        mesh=mesh,
        in_specs=(
            P(("dp", "expert"), None),
            P(("dp", "expert"), None),
            P(("dp", "expert"), None),
            P(("dp", "expert"), None),
            P("expert", "dp", None),
            P("expert", "dp", None),
            P("expert", None, "dp"),
        ),
        out_specs=(
            P(("dp", "expert"), None),
            P("expert", "dp", None),
            P("expert", "dp", None),
            P("expert", None, "dp"),
        ),
        check_vma=False,
    )
```

profile of v0, /device:TPU:1, one launch (start us, length us, event | category | flops | bytes accessed | tf_op | source)
XLA Modules:
  0.0 408.1 jit_solution(2590358224670452136)
XLA Ops:
  7.2 0.7 all-gather.8.cloned.1.call-update
  7.9 0.8 copy.14
  8.9 0.7 broadcast_multiply_fusion
  9.6 0.1 copy.13
  9.9 1.2 reduce-window.6
  11.1 0.2 slice_reduce_fusion
  11.3 0.1 fusion.19
  11.5 2.4 scatter_custom_fusion
  14.0 3.4 gather_fusion.2
  17.4 2.8 gather.19
  20.2 0.2 broadcast_in_dim.41
  20.4 4.5 %broadcast_select_fusion = bf16[64,9,2048]{2,1,0:T(8,128)(2,1)} fusion(bf16[64,9,2048]{2,1,0:T(8,128)(2,1)} %gather.19, pred[64,9]{1,0:T(8,128)(4,1)S(1)} %broadcast_in_dim.41), kind=kLoop, calls=%fused_computation.8 | loop fusion | flops 1179648 | bytes 4719168 | tf_op jit(solution)/shard_map/jit(_where)/select_n | solution.py:29
  24.9 13.2 %all-to-all-start.1 = ((bf16[64,9,2048]{2,1,0:T(8,128)(2,1)}), bf16[64,9,2048]{2,1,0:T(8,128)(2,1)}, u32[]{:S(2)}, u32[]{:S(2)}) async-start(bf16[64,9,2048]{2,1,0:T(8,128)(2,1)} %broadcast_select_fusion), calls=%async_computation.1 | async-start | bytes 8388608 | tf_op jit(solution)/shard_map/all_to_all | solution.py:35
  38.1 0.7 all-gather.6.cloned.1.call-update
  38.8 0.3 copy-done.2
  39.1 3.4 gather_fusion.1
  42.5 3.7 reshape.178
  46.5 4.0 gather_fusion
  50.5 0.1 mul.62
  50.6 5.2 %select_convert_fusion = bf16[64,9,2048]{2,1,0:T(8,128)(2,1)} fusion(f32[64,9,2048]{2,1,0:T(8,128)} %reshape.178, f32[64,9]{1,0:T(8,128)S(1)} %mul.62, pred[64,9]{1,0:T(8,128)(4,1)S(1)} %broadcast_in_dim.41), kind=kLoop, calls=%fused_computation.6 | loop fusion | flops 3538944 | bytes 7080768 | tf_op jit(solution)/shard_map/convert_element_type | solution.py:31
  55.8 78.2 %all-to-all-done.1 = bf16[64,9,2048]{2,1,0:T(8,128)(2,1)} async-done(((bf16[64,9,2048]{2,1,0:T(8,128)(2,1)}), bf16[64,9,2048]{2,1,0:T(8,128)(2,1)}, u32[]{:S(2)}, u32[]{:S(2)}) %all-to-all-start.1) | async-done | bytes 2359328 | tf_op jit(solution)/shard_map/all_to_all | solution.py:35
  134.0 5.9 %all-to-all-start = ((bf16[64,9,2048]{2,1,0:T(8,128)(2,1)}), bf16[64,9,2048]{2,1,0:T(8,128)(2,1)}, u32[]{:S(2)}, u32[]{:S(2)}) async-start(bf16[64,9,2048]{2,1,0:T(8,128)(2,1)} %select_convert_fusion), calls=%async_computation | async-start | bytes 8388608 | tf_op jit(solution)/shard_map/all_to_all | solution.py:36
  140.0 0.7 all-gather.4.cloned.1.call-update
  140.6 0.2 reduce-scatter.2.cloned.1.call-start
  140.9 3.4 reshape.171
  144.3 91.5 %all-to-all-done = bf16[64,9,2048]{2,1,0:T(8,128)(2,1)} async-done(((bf16[64,9,2048]{2,1,0:T(8,128)(2,1)}), bf16[64,9,2048]{2,1,0:T(8,128)(2,1)}, u32[]{:S(2)}, u32[]{:S(2)}) %all-to-all-start) | async-done | bytes 2359328 | tf_op jit(solution)/shard_map/all_to_all | solution.py:36
  235.8 4.7 %reshape.169 = bf16[576,2048]{1,0:T(8,128)(2,1)} reshape(bf16[64,9,2048]{2,1,0:T(8,128)(2,1)} %all-to-all-done) | data formatting | bytes 4718592 | tf_op jit(solution)/shard_map/reshape.3
  240.5 5.1 %fusion.2 = f32[576,768]{1,0:T(8,128)} fusion(bf16[576,2048]{1,0:T(8,128)(2,1)S(1)} %reshape.171, bf16[1,2048,768]{2,1,0:T(8,128)(2,1)} %all-gather.8.cloned.1.call-done), kind=kOutput, calls=%fused_computation.14 | convolution fusion | flops 1811939328 | bytes 7274496 | tf_op jit(solution)/shard_map/asd,adf->asf/dot_general | solution.py:46
  245.6 4.0 fusion.6
  249.6 1.3 copy-done.10
  250.9 4.1 %fusion.12 = bf16[2048,768]{0,1:T(8,128)(2,1)} fusion(bf16[576,2048]{1,0:T(8,128)(2,1)S(1)} %copy-done.4, f32[576,768]{1,0:T(8,128)S(1)} %fusion.6, f32[576,768]{1,0:T(8,128)S(1)} %copy-done.9), kind=kOutput, calls=%fused_computation.24 | convolution fusion | flops 1816166400 | bytes 9043968 | tf_op jit(solution)/shard_map/asd,asf->daf/dot_general | solution.py:89
  255.0 6.1 %multiply_convert_fusion.1 = (bf16[576,768]{1,0:T(8,128)(2,1)S(1)}, bf16[576,768]{1,0:T(8,128)(2,1)S(1)}) fusion(f32[576,768]{1,0:T(8,128)} %fusion.2, f32[576,768]{1,0:T(8,128)} %copy-done.10, bf16[576,2048]{1,0:T(8,128)(2,1)} %reshape.169, bf16[1,768,2048]{2,1,0:T(8,128)(2,1)} %all-gather.4.cloned.1.call-done), kind=kOutput, calls=%fused_computation.26 | convolution fusion | flops 1817690112 | bytes 10813440 | tf_op jit(solution)/shard_map/asd,afd->asf/dot_general | solution.py:66
  261.1 2.9 fusion.11
  264.1 2.9 fusion.10
  266.9 4.5 %pad_maximum_fusion = bf16[2048,2304]{0,1:T(8,128)(2,1)} fusion(bf16[2048,768]{0,1:T(8,128)(2,1)S(1)} %copy-done.3, bf16[2048,768]{0,1:T(8,128)(2,1)S(1)} %fusion.11, bf16[2048,768]{0,1:T(8,128)(2,1)S(1)} %fusion.10), kind=kLoop, calls=%fused_computation.5 | loop fusion | flops 28311552 | bytes 18874368 | tf_op jit(solution)/shard_map/concatenate | solution.py:91
  271.4 1.1 copy-done.8
  272.6 4.1 fusion
  276.7 2.0 add_convert_fusion
  278.7 2.8 reshape_transpose_reshape.2
  281.6 5.9 %all-to-all-start.2 = ((bf16[64,9,2048]{2,1,0:T(8,128)(2,1)}), bf16[64,9,2048]{2,1,0:T(8,128)(2,1)}, u32[]{:S(2)}, u32[]{:S(2)}) async-start(bf16[64,9,2048]{2,1,0:T(8,128)(2,1)} %reshape_transpose_reshape.2), calls=%async_computation.2 | async-start | bytes 8388608 | tf_op jit(solution)/shard_map/all_to_all | solution.py:79
  287.4 95.9 %all-to-all-done.2 = bf16[64,9,2048]{2,1,0:T(8,128)(2,1)} async-done(((bf16[64,9,2048]{2,1,0:T(8,128)(2,1)}), bf16[64,9,2048]{2,1,0:T(8,128)(2,1)}, u32[]{:S(2)}, u32[]{:S(2)}) %all-to-all-start.2) | async-done | bytes 2359328 | tf_op jit(solution)/shard_map/all_to_all | solution.py:79
  383.3 3.4 reshape.174
  386.7 3.3 gather_fusion.3
  390.0 2.7 gather.21
  392.7 3.9 reduce_sum.25
  396.6 2.7 slice_bitcast_fusion
  399.3 1.2 copy.18
  400.4 1.2 copy.19
  (45 shorter events, 0.8 us)
Async XLA Ops:
  7.2 6.8 %copy-start = (bf16[128,2048]{1,0:T(8,128)(2,1)S(1)}, bf16[128,2048]{1,0:T(8,128)(2,1)}, u32[]{:S(2)}) copy-start(bf16[128,2048]{1,0:T(8,128)(2,1)} %param.7) | copy-start | bytes 1572868
  7.2 233.3 %all-gather.8.cloned.1.call-start = ((), (), s32[]{:S(2)}) async-start(), calls=%async_computation.6 | async-start | bytes 3932160 | tf_op jit(solution)/shard_map/all_gather | solution.py:49
  24.9 109.1 %all-to-all-start.1 = ((bf16[64,9,2048]{2,1,0:T(8,128)(2,1)}), bf16[64,9,2048]{2,1,0:T(8,128)(2,1)}, u32[]{:S(2)}, u32[]{:S(2)}) async-start(bf16[64,9,2048]{2,1,0:T(8,128)(2,1)} %broadcast_select_fusion), calls=%async_computation.1 | async-start | bytes 8388608 | tf_op jit(solution)/shard_map/all_to_all | solution.py:35
  38.1 1.0 copy-start.2
  38.1 207.5 %all-gather.6.cloned.1.call-start = ((), (), s32[]{:S(2)}) async-start(), calls=%async_computation.5 | async-start | bytes 3932160 | tf_op jit(solution)/shard_map/all_gather | solution.py:55
  42.5 3.7 copy-start.5
  134.0 101.8 %all-to-all-start = ((bf16[64,9,2048]{2,1,0:T(8,128)(2,1)}), bf16[64,9,2048]{2,1,0:T(8,128)(2,1)}, u32[]{:S(2)}, u32[]{:S(2)}) async-start(bf16[64,9,2048]{2,1,0:T(8,128)(2,1)} %select_convert_fusion), calls=%async_computation | async-start | bytes 8388608 | tf_op jit(solution)/shard_map/all_to_all | solution.py:36
  139.9 115.1 %all-gather.4.cloned.1.call-start = ((), (), s32[]{:S(2)}) async-start(), calls=%async_computation.4 | async-start | bytes 3932160 | tf_op jit(solution)/shard_map/all_gather | solution.py:61
  140.6 255.9 %reduce-scatter.2.cloned.1.call-start = ((), (), s32[]{:S(2)}) async-start(), calls=%async_computation.7 | async-start | bytes 11796480 | tf_op jit(solution)/shard_map/reduce_scatter | solution.py:90
  245.6 5.4 %copy-start.4 = (bf16[576,2048]{1,0:T(8,128)(2,1)S(1)}, bf16[576,2048]{1,0:T(8,128)(2,1)}, u32[]{:S(2)}) copy-start(bf16[576,2048]{1,0:T(8,128)(2,1)} %reshape.169) | copy-start | bytes 7077892
  245.6 5.4 %copy-start.9 = (f32[576,768]{1,0:T(8,128)S(1)}, f32[576,768]{1,0:T(8,128)}, u32[]{:S(2)}) copy-start(f32[576,768]{1,0:T(8,128)} %fusion.2) | copy-start | bytes 5308420
  249.6 1.3 copy-start.10
  261.1 2.9 copy-start.11
  261.1 2.9 copy-start.7
  264.0 2.9 copy-start.3
  271.4 1.2 copy-start.8
  272.6 4.1 copy-start.6
  272.6 4.1 %copy-start.12 = (bf16[576,768]{1,0:T(8,128)(2,1)S(1)}, bf16[576,768]{1,0:T(8,128)(2,1)}, u32[]{:S(2)}) copy-start(bf16[576,768]{1,0:T(8,128)(2,1)} %copy-done.11) | copy-start | bytes 2654212
  281.6 101.8 %all-to-all-start.2 = ((bf16[64,9,2048]{2,1,0:T(8,128)(2,1)}), bf16[64,9,2048]{2,1,0:T(8,128)(2,1)}, u32[]{:S(2)}, u32[]{:S(2)}) async-start(bf16[64,9,2048]{2,1,0:T(8,128)(2,1)} %reshape_transpose_reshape.2), calls=%async_computation.2 | async-start | bytes 8388608 | tf_op jit(solution)/shard_map/all_to_all | solution.py:79
  396.6 5.0 %copy-start.1 = (bf16[128,2048]{1,0:T(8,128)(2,1)S(1)}, bf16[128,2048]{1,0:T(8,128)(2,1)}, u32[]{:S(2)}) copy-start(bf16[128,2048]{1,0:T(8,128)(2,1)} %param.7) | copy-start | bytes 1572868
Sparse Core Ops, SparseCore 0:
  9.8 45.9 all-gather.7
  57.6 42.3 all-gather.5
  142.6 43.2 all-gather.3
  271.6 88.2 reduce-scatter.1
where the time goes:
time: 409 us; the launch traced here: 408 us
  waiting for transfers between devices  268 us (66%)
  local copies, waits for them, and re-layouts  49.8 us (12%)
  matrix products  31.1 us (8%)
  starting transfers between devices  25.3 us (6%)
  other arithmetic  20.1 us (5%)
  between operations  14.1 us (3%)
    all_to_all x1, waiting for transfers between devices, local(): lax.all_to_all(send_back, 'expert', split_axis=0, concat_axis=0, tiled=True)  95.9 us
    all_to_all x1, waiting for transfers between devices, local(): lax.all_to_all(send_dy, 'expert', split_axis=0, concat_axis=0, tiled=True)  91.5 us
    all_to_all x1, waiting for transfers between devices, local(): lax.all_to_all(send_x, 'expert', split_axis=0, concat_axis=0, tiled=True)  78.2 us
    all_to_all x1, starting transfers between devices, local(): lax.all_to_all(send_x, 'expert', split_axis=0, concat_axis=0, tiled=True)  13.2 us
  transfers between devices with their start and end apart: 7, of which 3 were waited for; matrix products, arithmetic and copies ran while one was open for 19% of the time, Pallas kernels for 0%

commit v1 on v0

v1 whole, which is shorter than its diff:
```python
import jax
import jax.numpy as jnp
from jax import lax
from jax.experimental import pallas as pl
from jax.experimental.pallas import tpu as pltpu
from jax.sharding import PartitionSpec as P

MESH = pl.DeviceIdType.MESH
BF, F32 = jnp.bfloat16, jnp.float32
NY, NZ, NC = 4, 8, 2
ND = 8
TOK, D, FF, CAP = 128, 2048, 768, 9
ROWS = 80
SLOTS = ND * ROWS
Q = 512
NQ = D // Q
RING = NZ * TOK


def dot(a, b, dims):
    return lax.dot_general(a, b, (dims, ((), ())), preferred_element_type=F32)


NN = ((1,), (0,))
NT = ((1,), (1,))
TN = ((0,), (0,))


def kernel(
    tok, og, routes, gates, wg, wu, wd, ig_out, gg_out, ug_out, dg_out,
    ring, meta_s, meta_r, pick, gcol, sx, rx, rb, fg, fu, fd, act, up, back,
    active_bf, d_gate, d_up, p_gate, p_up, p_down, h_gate, h_up, h_down, s_gate, s_up, s_down,
    zr, ig,
    z_s, z_r, x_s, x_r, m_s, m_r, y_s, y_r, g_s, g_r, b_s, b_r, r_s, r_r, l_t, l_w, l_o,
):
    me = lax.axis_index("dp")
    e = lax.axis_index("expert")
    x, z, c = e // 16, (e // 2) % 8, e % 2
    d = x * 2 + c
    z_right, z_left = (z + 1) % NZ, (z + NZ - 1) % NZ
    y_right, y_left, y_far = (me + 1) % NY, (me + 3) % NY, (me + 2) % NY

    def at_z(k):
        return (me, x * 16 + k * 2 + c)

    def at_d(k):
        return (me, (k // 2) * 16 + z * 2 + k % 2)

    def at_y(k):
        return (k, e)

    def remote(src, dst, s, r, dev):
        return pltpu.make_async_remote_copy(
            src_ref=src, dst_ref=dst, send_sem=s, recv_sem=r, device_id=dev, device_id_type=MESH
        )

    barrier = pltpu.get_barrier_semaphore()
    for k in (y_right, y_left):
        pl.semaphore_signal(barrier, inc=1, device_id=at_y(k), device_id_type=MESH)
    for i in range(1, NZ):
        pl.semaphore_signal(barrier, inc=1, device_id=at_z((z + i) % NZ), device_id_type=MESH)
    for i in range(1, ND):
        pl.semaphore_signal(barrier, inc=1, device_id=at_d((d + i) % ND), device_id_type=MESH)
    pl.semaphore_wait(barrier, 2 + NZ - 1 + ND - 1)

    def own_chunk(k):
        return (tok if k < NQ else og).at[:, pl.ds((k % NQ) * Q, Q)]

    def z_has(k, s, way):
        return s < 3 or way == k % 2

    def z_copy(k, s, way):
        block = (z + NZ - s) % NZ if way == 0 else (z + s) % NZ
        src = own_chunk(k) if s == 0 else ring.at[k, block]
        n = (k * 4 + s) * 2 + way
        return remote(
            src, ring.at[k, block], z_s.at[n], z_r.at[n], at_z(z_right if way == 0 else z_left)
        )

    for k in range(2):
        for way in range(2):
            z_copy(k, 0, way).start()

    shards, fulls = (wg, wu, wd), (fg, fu, fd)

    def y_copy(kind, n):
        own, full = shards[kind], fulls[kind]
        half = own.shape[0] // 2
        low, high = pl.ds(0, half), pl.ds(half, half)
        sems = (y_s.at[kind * 6 + n], y_r.at[kind * 6 + n])
        if n < 4:
            part = low if n in (0, 3) else high
            return remote(own.at[part], full.at[me, part], *sems, at_y(y_right if n in (0, 2) else y_left))
        if n == 4:
            return remote(full.at[y_left, low], full.at[y_left, low], *sems, at_y(y_right))
        return remote(full.at[y_right, high], full.at[y_right, high], *sems, at_y(y_left))

    def y_begin(kind):
        for n in range(4):
            y_copy(kind, n).start()

    def y_forward(kind):
        y_copy(kind, 0).wait_recv()
        y_copy(kind, 4).start()
        y_copy(kind, 1).wait_recv()
        y_copy(kind, 5).start()

    def y_end(kind):
        for n in (2, 3, 4, 5):
            y_copy(kind, n).wait_recv()
        pltpu.make_async_copy(shards[kind], fulls[kind].at[me], l_w.at[kind]).wait()

    y_begin(0)
    for k in range(2 * NQ):
        pltpu.make_async_copy(own_chunk(k), ring.at[k, z], l_t.at[k]).start()
    for kind in range(3):
        pltpu.make_async_copy(shards[kind], fulls[kind].at[me], l_w.at[kind]).start()

    row = lax.broadcasted_iota(jnp.int32, (64, TOK), 0)
    expert = ((row % 8) // 2) * 16 + (row // 8) * 2 + row % 2
    chosen = jnp.zeros((64, TOK), F32)
    weight = jnp.zeros((64, TOK), F32)
    for k in range(4):
        hit = routes[pl.ds(k, 1), :] == expert
        chosen = chosen + jnp.where(hit, 1.0, 0.0)
        weight = weight + jnp.where(hit, gates[pl.ds(k, 1), :], 0.0)
    earlier = (
        lax.broadcasted_iota(jnp.int32, (TOK, TOK), 0) < lax.broadcasted_iota(jnp.int32, (TOK, TOK), 1)
    )
    before = dot(chosen.astype(BF), jnp.where(earlier, 1.0, 0.0).astype(BF), NN)
    slot = jnp.where(chosen > 0.0, before, -1000.0)
    for k in range(NZ):
        meta_s[k, 0:8, :] = slot[k * 8 : k * 8 + 8, :]
        meta_s[k, 8:16, :] = weight[k * 8 : k * 8 + 8, :]

    def m_copy(i):
        to = (z + i) % NZ
        return remote(meta_s.at[to], meta_r.at[z], m_s.at[i], m_r.at[i], at_z(to))

    for i in range(1, NZ):
        m_copy(i).start()
    meta_r[z] = meta_s[z]

    def build_pick():
        for i in range(1, NZ):
            m_copy(i).wait_recv()
        ids = lax.broadcasted_iota(jnp.int32, (ROWS, TOK), 0).astype(F32)

        def one(k, _):
            rows = pl.ds(pl.multiple_of(k * ROWS, 16), ROWS)
            scale = jnp.zeros((ROWS, 1), F32)
            for zz in range(NZ):
                wanted = meta_r[zz, pl.ds(k, 1), :] + float(zz * CAP)
                hit = ids == wanted
                pick[rows, zz * TOK : (zz + 1) * TOK] = jnp.where(hit, 1.0, 0.0).astype(BF)
                gate = jnp.where(hit, meta_r[zz, pl.ds(k + 8, 1), :], 0.0)
                scale = scale + jnp.sum(gate, axis=1, keepdims=True)
            gcol[rows, :] = jnp.broadcast_to(scale, (ROWS, TOK))
            return 0

        lax.fori_loop(0, ND, one, 0)

    mine = pl.ds(pl.multiple_of(d * ROWS, 16), ROWS)

    def x_copy(k, i):
        to = (d + i) % ND
        src = sx.at[k, pl.ds(pl.multiple_of(to * ROWS, 16), ROWS)]
        n = k * 8 + i
        return remote(src, rx.at[k, mine], x_s.at[n], x_r.at[n], at_d(to))

    def gather(k):
        def one(n, _):
            cols = pl.ds(pl.multiple_of(n * 256, 256), 256)
            got = dot(pick[...], ring[k, :, :, cols].reshape(RING, 256), NN)
            if k >= NQ:
                got = got * gcol[:, 0:1]
            sx[k, :, cols] = got.astype(BF)
            return 0

        lax.fori_loop(0, 2, one, 0)
        for i in range(1, ND):
            x_copy(k, i).start()
        rx[k, mine, :] = sx[k, mine, :]

    def x_end(k):
        for i in range(1, ND):
            x_copy(k, i).wait_recv()

    def first_matmuls(pair):
        for k in (2 * pair, 2 * pair + 1):
            x_end(k)

        def one(n, _):
            cols = pl.ds(pl.multiple_of(n * 256, 256), 256)
            for full, into in ((fg, act), (fu, up)):
                got = dot(rx[2 * pair], full[2 * pair, :, cols], NN)
                got = got + dot(rx[2 * pair + 1], full[2 * pair + 1, :, cols], NN)
                into[:, cols] = got if pair == 0 else into[:, cols] + got
            return 0

        lax.fori_loop(0, 3, one, 0)

    def activations():
        def one(n, _):
            rows = pl.ds(pl.multiple_of(n * 32, 32), 32)
            g, u = act[rows, :], up[rows, :]
            sigma = jax.nn.sigmoid(g)
            silu = g * sigma
            active_bf[rows, :] = (silu * u).astype(BF)
            act[rows, :] = silu
            up[rows, :] = u * sigma * (1.0 + g * (1.0 - sigma))
            return 0

        lax.fori_loop(0, SLOTS // 32, one, 0)

    def back_matmul(pair):
        for k in (2 * pair, 2 * pair + 1):
            x_end(NQ + k)

        def one(n, _):
            cols = pl.ds(pl.multiple_of(n * 256, 256), 256)
            got = dot(rx[NQ + 2 * pair], fd[2 * pair, cols, :], NT)
            got = got + dot(rx[NQ + 2 * pair + 1], fd[2 * pair + 1, cols, :], NT)
            back[:, cols] = got if pair == 0 else back[:, cols] + got
            return 0

        lax.fori_loop(0, 3, one, 0)

    def deltas():
        def one(n, _):
            rows = pl.ds(pl.multiple_of(n * 32, 32), 32)
            b = back[rows, :]
            d_up[rows, :] = (b * act[rows, :]).astype(BF)
            d_gate[rows, :] = (b * up[rows, :]).astype(BF)
            return 0

        lax.fori_loop(0, SLOTS // 32, one, 0)

    for pair in range(NQ):
        for s in range(4):
            for k in (2 * pair, 2 * pair + 1):
                if s > 0:
                    for way in range(2):
                        z_copy(k, s - 1, way).wait_recv()
                        if z_has(k, s, way):
                            z_copy(k, s, way).start()
            if pair == 0 and s == 0:
                build_pick()
            if pair == 0 and s == 2:
                y_forward(0)
                y_begin(1)
            if pair == 1 and s == 3:
                y_forward(1)
                y_begin(2)
            if pair == 3 and s == 0:
                y_forward(2)
            if pair == 2 and s == 2:
                y_end(0)
                y_end(1)
                first_matmuls(0)
            if pair == 3 and s == 1:
                first_matmuls(1)
            if pair == 3 and s == 2:
                activations()
        if pair < NQ - 1:
            for k in (2 * pair + 2, 2 * pair + 3):
                for way in range(2):
                    z_copy(k, 0, way).start()
        z_copy(2 * pair, 3, 0).wait_recv()
        z_copy(2 * pair + 1, 3, 1).wait_recv()
        for k in (2 * pair, 2 * pair + 1):
            pltpu.make_async_copy(own_chunk(k), ring.at[k, z], l_t.at[k]).wait()
            gather(k)
    y_end(2)
    back_matmul(0)
    back_matmul(1)
    deltas()

    for k in range(2 * NQ):
        for s in range(4):
            for way in range(2):
                if z_has(k, s, way):
                    z_copy(k, s, way).wait_send()
    for k in range(NQ):
        for i in range(1, ND):
            x_copy(k, i).wait_send()

    parts, halves, sums = (p_down, p_gate, p_up), (h_down, h_gate, h_up), (s_down, s_gate, s_up)

    def part(kind, b):
        if kind == 0:

            def one(n, _):
                cols = pl.ds(pl.multiple_of(n * 256, 256), 256)
                p_down[b, :, cols] = dot(active_bf[...], rx[NQ + b, :, cols], TN).astype(BF)
                return 0

            lax.fori_loop(0, 2, one, 0)
        else:
            into, delta = (p_gate, d_gate) if kind == 1 else (p_up, d_up)

            def one(n, _):
                cols = pl.ds(pl.multiple_of(n * 256, 256), 256)
                into[b, :, cols] = dot(rx[b], delta[:, cols], TN).astype(BF)
                return 0

            lax.fori_loop(0, 3, one, 0)

    def g_copy(kind, n):
        src, half, total = parts[kind], halves[kind], sums[kind]
        size = src.shape[1] // 2
        low, high = pl.ds(0, size), pl.ds(size, size)
        sems = (g_s.at[kind * 6 + n], g_r.at[kind * 6 + n])
        if n == 0:
            return remote(src.at[y_far, low], half.at[0], *sems, at_y(y_right))
        if n == 1:
            return remote(src.at[y_far, high], half.at[1], *sems, at_y(y_left))
        part_of = high if n in (2, 5) else low
        if n in (2, 4):
            return remote(src.at[y_right, part_of], total.at[0, part_of], *sems, at_y(y_right))
        return remote(src.at[y_left, part_of], total.at[1, part_of], *sems, at_y(y_left))

    def g_combine(kind):
        src, half = parts[kind], halves[kind]
        size = src.shape[1] // 2
        for way, to in ((0, y_right), (1, y_left)):
            g_copy(kind, way).wait_recv()
            where = pl.ds(way * size, size)
            mixed = src[to, where, :].astype(F32) + half[way].astype(F32)
            src[to, where, :] = mixed.astype(BF)
            g_copy(kind, 4 + way).start()

    for kind in range(3):
        part(kind, y_far)
        g_copy(kind, 0).start()
        g_copy(kind, 1).start()
    for kind in range(3):
        part(kind, y_right)
        g_copy(kind, 2).start()
        part(kind, y_left)
        g_copy(kind, 3).start()

    def b_copy(k, i):
        to = (d + i) % ND
        src = sx.at[k, pl.ds(pl.multiple_of(to * ROWS, 16), ROWS)]
        n = k * 8 + i
        return remote(src, rb.at[k, mine], b_s.at[n], b_r.at[n], at_d(to))

    def pair_grads(k):
        def one(n, _):
            rows = pl.ds(pl.multiple_of(n * 256, 256), 256)
            got = dot(d_gate[...], fg[k, rows, :], NT) + dot(d_up[...], fu[k, rows, :], NT)
            sx[k, :, rows] = got.astype(BF)
            return 0

        lax.fori_loop(0, 2, one, 0)
        for i in range(1, ND):
            b_copy(k, i).start()
        rb[k, mine, :] = sx[k, mine, :]

    for k in range(NQ):
        pair_grads(k)

    def token_sums(k):
        for i in range(1, ND):
            b_copy(k, i).wait_recv()

        def one(n, _):
            got = dot(pick[:, pl.ds(pl.multiple_of(n * TOK, TOK), TOK)], rb[k], TN)
            ring[k, n] = got.astype(BF)
            return 0

        lax.fori_loop(0, NZ, one, 0)

    def r_has(k, s, way):
        return s > 0 or way == k % 2

    def r_copy(k, s, way):
        block = (z + 4 + NZ - s) % NZ if way == 0 else (z + 4 + s) % NZ
        n = (k * 4 + s) * 2 + way
        return remote(
            ring.at[k, block], zr.at[n], r_s.at[n], r_r.at[n], at_z(z_right if way == 0 else z_left)
        )

    def r_send(k, s, way):
        if s > 0 and r_has(k, s - 1, way):
            block = (z + 4 + NZ - s) % NZ if way == 0 else (z + 4 + s) % NZ
            r_copy(k, s - 1, way).wait_recv()
            mixed = ring[k, block].astype(F32) + zr[(k * 4 + s - 1) * 2 + way].astype(F32)
            ring[k, block] = mixed.astype(BF)
        r_copy(k, s, way).start()

    def ring_sums(pair):
        for s in range(4):
            for k in (2 * pair, 2 * pair + 1):
                for way in range(2):
                    if r_has(k, s, way):
                        r_send(k, s, way)

    def tokens_out(pair):
        for k in (2 * pair, 2 * pair + 1):
            total = ring[k, z].astype(F32)
            for way in range(2):
                r_copy(k, 3, way).wait_recv()
                total = total + zr[(k * 4 + 3) * 2 + way].astype(F32)
            ig[:, k * Q : (k + 1) * Q] = total.astype(BF)

    token_sums(0)
    token_sums(1)
    ring_sums(0)
    for kind in range(3):
        g_combine(kind)
    token_sums(2)
    token_sums(3)
    tokens_out(0)
    ring_sums(1)
    for kind in range(3):
        part(kind, me)
    tokens_out(1)
    o_copy = pltpu.make_async_copy(ig, ig_out, l_o.at[3])
    o_copy.start()

    outs = (dg_out, gg_out, ug_out)
    for kind in range(3):
        src, total = parts[kind], sums[kind]
        for n in (2, 3, 4, 5):
            g_copy(kind, n).wait_recv()
        size = src.shape[1] // 4

        def one(n, _, src=src, total=total, size=size):
            rows = pl.ds(pl.multiple_of(n * size, 32), size)
            mixed = src[me, rows, :].astype(F32) + total[0, rows, :].astype(F32)
            src[me, rows, :] = (mixed + total[1, rows, :].astype(F32)).astype(BF)
            return 0

        lax.fori_loop(0, 4, one, 0)
        pltpu.make_async_copy(src.at[me], outs[kind], l_o.at[kind]).start()

    for kind in range(3):
        for n in range(6):
            y_copy(kind, n).wait_send()
            g_copy(kind, n).wait_send()
        pltpu.make_async_copy(parts[kind].at[me], outs[kind], l_o.at[kind]).wait()
    for i in range(1, NZ):
        m_copy(i).wait_send()
    for k in range(NQ):
        for i in range(1, ND):
            x_copy(NQ + k, i).wait_send()
            b_copy(k, i).wait_send()
        for s in range(4):
            for way in range(2):
                if r_has(k, s, way):
                    r_copy(k, s, way).wait_send()
    o_copy.wait()


def local(tokens, out_grad, routes, gate_values, w_gate, w_up, w_down):
    hbm = pl.BlockSpec(memory_space=pl.ANY)
    vmem = pl.BlockSpec(memory_space=pltpu.VMEM)
    sem = pltpu.SemaphoreType.DMA
    out = lambda *shape: jax.ShapeDtypeStruct(shape, BF)
    scratch = [
        pltpu.VMEM((2 * NQ, NZ, TOK, Q), BF),
        pltpu.VMEM((NZ, 16, TOK), F32),
        pltpu.VMEM((NZ, 16, TOK), F32),
        pltpu.VMEM((SLOTS, RING), BF),
        pltpu.VMEM((SLOTS, TOK), F32),
        pltpu.VMEM((2 * NQ, SLOTS, Q), BF),
        pltpu.VMEM((2 * NQ, SLOTS, Q), BF),
        pltpu.VMEM((NQ, SLOTS, Q), BF),
        pltpu.VMEM((NY, D // NY, FF), BF),
        pltpu.VMEM((NY, D // NY, FF), BF),
        pltpu.VMEM((NY, FF, D // NY), BF),
        pltpu.VMEM((SLOTS, FF), F32),
        pltpu.VMEM((SLOTS, FF), F32),
        pltpu.VMEM((SLOTS, FF), F32),
        pltpu.VMEM((SLOTS, FF), BF),
        pltpu.VMEM((SLOTS, FF), BF),
        pltpu.VMEM((SLOTS, FF), BF),
        pltpu.VMEM((NY, D // NY, FF), BF),
        pltpu.VMEM((NY, D // NY, FF), BF),
        pltpu.VMEM((NY, FF, D // NY), BF),
        pltpu.VMEM((2, D // NY // 2, FF), BF),
        pltpu.VMEM((2, D // NY // 2, FF), BF),
        pltpu.VMEM((2, FF // 2, D // NY), BF),
        pltpu.VMEM((2, D // NY, FF), BF),
        pltpu.VMEM((2, D // NY, FF), BF),
        pltpu.VMEM((2, FF, D // NY), BF),
        pltpu.VMEM((NQ * 8, TOK, Q), BF),
        pltpu.VMEM((TOK, D), BF),
        sem((64,)), sem((64,)), sem((64,)), sem((64,)), sem((8,)), sem((8,)), sem((18,)), sem((18,)),
        sem((18,)), sem((18,)), sem((32,)), sem((32,)), sem((32,)), sem((32,)), sem((8,)), sem((3,)), sem((4,)),
    ]
    return pl.pallas_call(
        kernel,
        out_shape=(out(TOK, D), out(D // NY, FF), out(D // NY, FF), out(FF, D // NY)),
        in_specs=[hbm, hbm, vmem, vmem, hbm, hbm, hbm],
        out_specs=(hbm, hbm, hbm, hbm),
        scratch_shapes=scratch,
        compiler_params=pltpu.CompilerParams(
            collective_id=0, has_side_effects=True, vmem_limit_bytes=66_000_000
        ),
    )(tokens, out_grad, routes.T, gate_values.T, w_gate[0], w_up[0], w_down[0])


def body(*arrays):
    ig, gg, ug, dg = local(*arrays)
    return ig, gg[None], ug[None], dg[None]


def solution(mesh):
    rows, experts = P(("dp", "expert"), None), P("expert", "dp", None)
    down = P("expert", None, "dp")
    return jax.shard_map(
        body,
        mesh=mesh,
        in_specs=(rows, rows, rows, rows, experts, experts, down),
        out_specs=(rows, experts, experts, down),
        check_vma=False,
    )
```

time: 409 us -> 210 us (0.51)
  waiting for transfers between devices: 268 us -> 0 us
  Pallas kernels: 0 us -> 203 us
  local copies, waits for them, and re-layouts: 49.8 us -> 5.67 us
  matrix products: 31.1 us -> 0 us
  starting transfers between devices: 25.3 us -> 0 us
  other arithmetic: 20.1 us -> 0 us
  between operations: 14.1 us -> 0.65 us
    all_to_all x3 -> x0, waiting for transfers between devices: 266 us -> none  [the longest x1 95.9 us: local(): lax.all_to_all(send_back, 'expert', split_axis=0, concat_axis=0, tiled=True)]
    pallas_call x0 -> x1, Pallas kernels: none -> 203 us  [local(): pl.pallas_call(kernel, out_shape=(out(TOK, D), out(D // NY, FF), out(D //...]
    dot_general x8 -> x0, matrix products: 31.1 us -> none  [the longest x1 6.08 us: local(): jnp.einsum('asd,afd->asf', slot_dy, full_down, preferred_element_type=jnp...]
    all_to_all x3 -> x0, starting transfers between devices: 25 us -> none  [the longest x1 13.2 us: local(): lax.all_to_all(send_x, 'expert', split_axis=0, concat_axis=0, tiled=True)]
    gather x6 -> x0, local copies, waits for them, and re-layouts: 19.6 us -> none  [the longest x2 6.23 us: local(): tokens[owner_row]]
    another operation x4 -> x0, local copies, waits for them, and re-layouts: 10.9 us -> none
    convert_element_type x2 -> x0, local copies, waits for them, and re-layouts: 6.42 us -> none  [the longest x1 3.72 us: local(): out_grad[owner_row].astype(jnp.float32)]
    convert_element_type x2 -> x0, other arithmetic: 5.21 us -> none  [the longest x1 5.2 us: local(): send_dy = jnp.where(filled[:, None], scaled, 0.0).astype(jnp.bfloat16)]
  transfers between devices with their start and end apart: 7 -> 0, of which waited for: 3 -> 0; matrix products, arithmetic and copies ran while one was open for 19% -> 0% of each run, Pallas kernels for 0% -> 0%
where the time goes in v1:
time: 210 us
  Pallas kernels  203 us (97%)
  local copies, waits for them, and re-layouts  5.67 us (3%)
    pallas_call x1, Pallas kernels, local(): pl.pallas_call(kernel, out_shape=(out(TOK, D), out(D // NY, FF), out(D //...  203 us
    unnamed x10, local copies, waits for them, and re-layouts  5.67 us

profile of v1, /device:TPU:1, one launch (start us, length us, event | category | flops | bytes accessed | tf_op | source)
XLA Modules:
  0.0 209.6 jit_solution(8912220697752523132)
XLA Ops:
  0.6 203.3 %shard_map.102 = (bf16[128,2048]{1,0:T(8,128)(2,1)}, bf16[512,768]{1,0:T(8,128)(2,1)}, bf16[512,768]{1,0:T(8,128)(2,1)}, bf16[768,512]{1,0:T(8,128)(2,1)}) custom-call(bf16[128,2048]{1,0:T(8,128)(2,1)} %tok.1, bf16[128,2048]{1,0:T(8,128)(2,1)} %og.1, s32[4,128]{1,0:T(4,128)} %bitcast.14, f32[4,128]{1,0:T(4,128)} %bitcast.15, bf16[512,768]{1,0:T(8,128)(2,1)} %bitcast.11, ...), custom_call_target="tpu_custom_call" | custom-call | tf_op jit(solution)/shard_map/pallas_call | solution.py:494
  204.0 0.0 copy-start.2
  204.0 2.0 copy.15
  205.9 0.0 copy-done.2
  205.9 0.0 copy-start.1
  205.9 0.9 copy.16
  206.8 0.5 copy-done.1
  207.3 0.0 copy-start
  207.3 0.9 copy.17
  208.2 0.5 copy-done
  208.8 0.9 copy.18
Async XLA Ops:
  204.0 2.0 copy-start.2
  205.9 1.4 copy-start.1
  207.3 1.4 copy-start

commit v2 on v1

--- a/solution.py
+++ b/solution.py
@@ -28,7 +28,7 @@
 
 def kernel(
     tok, og, routes, gates, wg, wu, wd, ig_out, gg_out, ug_out, dg_out,
-    ring, meta_s, meta_r, pick, gcol, sx, rx, rb, fg, fu, fd, act, up, back,
+    ring, meta_s, meta_r, pick, pick_t, gcol, sx, rx, rb, fg, fu, fd, act, up, back,
     active_bf, d_gate, d_up, p_gate, p_up, p_down, h_gate, h_up, h_down, s_gate, s_up, s_down,
     zr, ig,
     z_s, z_r, x_s, x_r, m_s, m_r, y_s, y_r, g_s, g_r, b_s, b_r, r_s, r_r, l_t, l_w, l_o,
@@ -63,8 +63,12 @@
         pl.semaphore_signal(barrier, inc=1, device_id=at_d((d + i) % ND), device_id_type=MESH)
     pl.semaphore_wait(barrier, 2 + NZ - 1 + ND - 1)
 
+    block_of = (y_far, y_right, y_left, me)
+
     def own_chunk(k):
-        return (tok if k < NQ else og).at[:, pl.ds((k % NQ) * Q, Q)]
+        if k < NQ:
+            return tok.at[:, pl.ds(k * Q, Q)]
+        return og.at[:, pl.ds(pl.multiple_of(block_of[k - NQ] * Q, Q), Q)]
 
     def z_has(k, s, way):
         return s < 3 or way == k % 2
@@ -77,9 +81,18 @@
             src, ring.at[k, block], z_s.at[n], z_r.at[n], at_z(z_right if way == 0 else z_left)
         )
 
-    for k in range(2):
+    def z_start(k):
         for way in range(2):
             z_copy(k, 0, way).start()
+
+    def z_step(k, s):
+        for way in range(2):
+            z_copy(k, s - 1, way).wait_recv()
+            if z_has(k, s, way):
+                z_copy(k, s, way).start()
+
+    z_start(0)
+    z_start(1)
 
     shards, fulls = (wg, wu, wd), (fg, fu, fd)
 
@@ -159,6 +172,9 @@
             return 0
 
         lax.fori_loop(0, ND, one, 0)
+        for zz in range(NZ):
+            cols = slice(zz * TOK, (zz + 1) * TOK)
+            pick_t[cols, :] = pick[:, cols].T
 
     mine = pl.ds(pl.multiple_of(d * ROWS, 16), ROWS)
 
@@ -169,6 +185,9 @@
         return remote(src, rx.at[k, mine], x_s.at[n], x_r.at[n], at_d(to))
 
     def gather(k):
+        z_copy(k, 3, k % 2).wait_recv()
+        pltpu.make_async_copy(own_chunk(k), ring.at[k, z], l_t.at[k]).wait()
+
         def one(n, _):
             cols = pl.ds(pl.multiple_of(n * 256, 256), 256)
             got = dot(pick[...], ring[k, :, :, cols].reshape(RING, 256), NN)
@@ -186,16 +205,12 @@
         for i in range(1, ND):
             x_copy(k, i).wait_recv()
 
-    def first_matmuls(pair):
-        for k in (2 * pair, 2 * pair + 1):
-            x_end(k)
-
+    def first_matmul(pair, full, into):
         def one(n, _):
             cols = pl.ds(pl.multiple_of(n * 256, 256), 256)
-            for full, into in ((fg, act), (fu, up)):
-                got = dot(rx[2 * pair], full[2 * pair, :, cols], NN)
-                got = got + dot(rx[2 * pair + 1], full[2 * pair + 1, :, cols], NN)
-                into[:, cols] = got if pair == 0 else into[:, cols] + got
+            got = dot(rx[2 * pair], full[2 * pair, :, cols], NN)
+            got = got + dot(rx[2 * pair + 1], full[2 * pair + 1, :, cols], NN)
+            into[:, cols] = got if pair == 0 else into[:, cols] + got
             return 0
 
         lax.fori_loop(0, 3, one, 0)
@@ -213,15 +228,11 @@
 
         lax.fori_loop(0, SLOTS // 32, one, 0)
 
-    def back_matmul(pair):
-        for k in (2 * pair, 2 * pair + 1):
-            x_end(NQ + k)
-
+    def back_matmul(i):
         def one(n, _):
             cols = pl.ds(pl.multiple_of(n * 256, 256), 256)
-            got = dot(rx[NQ + 2 * pair], fd[2 * pair, cols, :], NT)
-            got = got + dot(rx[NQ + 2 * pair + 1], fd[2 * pair + 1, cols, :], NT)
-            back[:, cols] = got if pair == 0 else back[:, cols] + got
+            got = dot(rx[NQ + i], fd[block_of[i], cols, :], NT)
+            back[:, cols] = got if i == 0 else back[:, cols] + got
             return 0
 
         lax.fori_loop(0, 3, one, 0)
@@ -236,63 +247,15 @@
 
         lax.fori_loop(0, SLOTS // 32, one, 0)
 
-    for pair in range(NQ):
-        for s in range(4):
-            for k in (2 * pair, 2 * pair + 1):
-                if s > 0:
-                    for way in range(2):
-                        z_copy(k, s - 1, way).wait_recv()
-                        if z_has(k, s, way):
-                            z_copy(k, s, way).start()
-            if pair == 0 and s == 0:
-                build_pick()
-            if pair == 0 and s == 2:
-                y_forward(0)
-                y_begin(1)
-            if pair == 1 and s == 3:
-                y_forward(1)
-                y_begin(2)
-            if pair == 3 and s == 0:
-                y_forward(2)
-            if pair == 2 and s == 2:
-                y_end(0)
-                y_end(1)
-                first_matmuls(0)
-            if pair == 3 and s == 1:
-                first_matmuls(1)
-            if pair == 3 and s == 2:
-                activations()
-        if pair < NQ - 1:
-            for k in (2 * pair + 2, 2 * pair + 3):
-                for way in range(2):
-                    z_copy(k, 0, way).start()
-        z_copy(2 * pair, 3, 0).wait_recv()
-        z_copy(2 * pair + 1, 3, 1).wait_recv()
-        for k in (2 * pair, 2 * pair + 1):
-            pltpu.make_async_copy(own_chunk(k), ring.at[k, z], l_t.at[k]).wait()
-            gather(k)
-    y_end(2)
-    back_matmul(0)
-    back_matmul(1)
-    deltas()
-
-    for k in range(2 * NQ):
-        for s in range(4):
-            for way in range(2):
-                if z_has(k, s, way):
-                    z_copy(k, s, way).wait_send()
-    for k in range(NQ):
-        for i in range(1, ND):
-            x_copy(k, i).wait_send()
-
     parts, halves, sums = (p_down, p_gate, p_up), (h_down, h_gate, h_up), (s_down, s_gate, s_up)
 
-    def part(kind, b):
+    def part(kind, i):
+        b = block_of[i]
         if kind == 0:
 
             def one(n, _):
                 cols = pl.ds(pl.multiple_of(n * 256, 256), 256)
-                p_down[b, :, cols] = dot(active_bf[...], rx[NQ + b, :, cols], TN).astype(BF)
+                p_down[b, :, cols] = dot(active_bf[...], rx[NQ + i, :, cols], TN).astype(BF)
                 return 0
 
             lax.fori_loop(0, 2, one, 0)
@@ -330,15 +293,9 @@
             src[to, where, :] = mixed.astype(BF)
             g_copy(kind, 4 + way).start()
 
-    for kind in range(3):
-        part(kind, y_far)
+    def g_begin(kind):
         g_copy(kind, 0).start()
         g_copy(kind, 1).start()
-    for kind in range(3):
-        part(kind, y_right)
-        g_copy(kind, 2).start()
-        part(kind, y_left)
-        g_copy(kind, 3).start()
 
     def b_copy(k, i):
         to = (d + i) % ND
@@ -358,19 +315,17 @@
             b_copy(k, i).start()
         rb[k, mine, :] = sx[k, mine, :]
 
-    for k in range(NQ):
-        pair_grads(k)
-
     def token_sums(k):
         for i in range(1, ND):
             b_copy(k, i).wait_recv()
 
         def one(n, _):
-            got = dot(pick[:, pl.ds(pl.multiple_of(n * TOK, TOK), TOK)], rb[k], TN)
-            ring[k, n] = got.astype(BF)
-            return 0
-
-        lax.fori_loop(0, NZ, one, 0)
+            rows = pl.ds(pl.multiple_of(n * 4 * TOK, 4 * TOK), 4 * TOK)
+            got = dot(pick_t[rows, :], rb[k], NN)
+            ring[k, pl.ds(n * 4, 4)] = got.astype(BF).reshape(4, TOK, Q)
+            return 0
+
+        lax.fori_loop(0, NZ // 4, one, 0)
 
     def r_has(k, s, way):
         return s > 0 or way == k % 2
@@ -390,33 +345,139 @@
             ring[k, block] = mixed.astype(BF)
         r_copy(k, s, way).start()
 
-    def ring_sums(pair):
+    def ring_step(k, s):
+        for way in range(2):
+            if r_has(k, s, way):
+                r_send(k, s, way)
+
+    def tokens_out(k):
+        total = ring[k, z].astype(F32)
+        for way in range(2):
+            r_copy(k, 3, way).wait_recv()
+            total = total + zr[(k * 4 + 3) * 2 + way].astype(F32)
+        ig[:, k * Q : (k + 1) * Q] = total.astype(BF)
+
+    z_step(0, 1)
+    z_step(1, 1)
+    z_start(2)
+    y_begin(1)
+    z_step(0, 2)
+    z_step(1, 2)
+    build_pick()
+    z_step(0, 3)
+    z_step(1, 3)
+    z_start(3)
+    z_start(4)
+    y_forward(0)
+    gather(0)
+    gather(1)
+    for k in (2, 3, 4):
+        z_step(k, 1)
+    for k in (2, 3, 4):
+        z_step(k, 2)
+    y_begin(2)
+    for k in (2, 3, 4):
+        z_step(k, 3)
+    z_start(5)
+    z_start(6)
+    y_forward(1)
+    gather(2)
+    gather(3)
+    gather(4)
+    z_step(5, 1)
+    z_step(6, 1)
+    z_start(7)
+    y_end(0)
+    x_end(0)
+    x_end(1)
+    first_matmul(0, fg, act)
+    z_step(5, 2)
+    z_step(6, 2)
+    x_end(2)
+    x_end(3)
+    first_matmul(1, fg, act)
+    z_step(7, 1)
+    z_step(5, 3)
+    z_step(6, 3)
+    y_end(1)
+    first_matmul(0, fu, up)
+    y_forward(2)
+    gather(5)
+    gather(6)
+    z_step(7, 2)
+    first_matmul(1, fu, up)
+    z_step(7, 3)
+    activations()
+    x_end(4)
+    part(0, 0)
+    g_begin(0)
+    gather(7)
+    x_end(5)
+    part(0, 1)
+    g_copy(0, 2).start()
+    y_end(2)
+    back_matmul(0)
+    back_matmul(1)
+    x_end(6)
+    part(0, 2)
+    g_copy(0, 3).start()
+    back_matmul(2)
+    g_combine(0)
+    x_end(7)
+    back_matmul(3)
+    deltas()
+
+    for k in range(NQ):
         for s in range(4):
-            for k in (2 * pair, 2 * pair + 1):
-                for way in range(2):
-                    if r_has(k, s, way):
-                        r_send(k, s, way)
-
-    def tokens_out(pair):
-        for k in (2 * pair, 2 * pair + 1):
-            total = ring[k, z].astype(F32)
             for way in range(2):
-                r_copy(k, 3, way).wait_recv()
-                total = total + zr[(k * 4 + 3) * 2 + way].astype(F32)
-            ig[:, k * Q : (k + 1) * Q] = total.astype(BF)
-
+                if z_has(k, s, way):
+                    z_copy(k, s, way).wait_send()
+        for i in range(1, ND):
+            x_copy(k, i).wait_send()
+
+    pair_grads(0)
+    pair_grads(1)
+    part(1, 0)
+    g_begin(1)
+    pair_grads(2)
+    part(2, 0)
+    g_begin(2)
+    pair_grads(3)
+    part(1, 1)
+    g_copy(1, 2).start()
     token_sums(0)
+    ring_step(0, 0)
+    ring_step(0, 1)
+    part(1, 2)
+    g_copy(1, 3).start()
     token_sums(1)
-    ring_sums(0)
-    for kind in range(3):
-        g_combine(kind)
+    ring_step(1, 0)
+    part(2, 1)
+    g_copy(2, 2).start()
+    ring_step(0, 2)
+    ring_step(1, 1)
+    part(2, 2)
+    g_copy(2, 3).start()
+    g_combine(1)
+    ring_step(0, 3)
+    ring_step(1, 2)
     token_sums(2)
+    ring_step(2, 0)
+    ring_step(2, 1)
+    ring_step(1, 3)
+    g_combine(2)
     token_sums(3)
-    tokens_out(0)
-    ring_sums(1)
-    for kind in range(3):
-        part(kind, me)
-    tokens_out(1)
+    ring_step(3, 0)
+    ring_step(2, 2)
+    ring_step(3, 1)
+    part(0, 3)
+    ring_step(2, 3)
+    ring_step(3, 2)
+    part(1, 3)
+    ring_step(3, 3)
+    part(2, 3)
+    for k in range(NQ):
+        tokens_out(k)
     o_copy = pltpu.make_async_copy(ig, ig_out, l_o.at[3])
     o_copy.start()
 
@@ -449,6 +510,8 @@
             b_copy(k, i).wait_send()
         for s in range(4):
             for way in range(2):
+                if z_has(NQ + k, s, way):
+                    z_copy(NQ + k, s, way).wait_send()
                 if r_has(k, s, way):
                     r_copy(k, s, way).wait_send()
     o_copy.wait()
@@ -464,6 +527,7 @@
         pltpu.VMEM((NZ, 16, TOK), F32),
         pltpu.VMEM((NZ, 16, TOK), F32),
         pltpu.VMEM((SLOTS, RING), BF),
+        pltpu.VMEM((RING, SLOTS), BF),
         pltpu.VMEM((SLOTS, TOK), F32),
         pltpu.VMEM((2 * NQ, SLOTS, Q), BF),
         pltpu.VMEM((2 * NQ, SLOTS, Q), BF),

time: 210 us -> 190 us (0.905)
  Pallas kernels: 203 us -> 184 us
    pallas_call x1, Pallas kernels: 203 us -> 184 us  [local(): pl.pallas_call(kernel, out_shape=(out(TOK, D), out(D // NY, FF), out(D //...]
where the time goes in v2:
time: 190 us
  Pallas kernels  184 us (97%)
  local copies, waits for them, and re-layouts  5.67 us (3%)
    pallas_call x1, Pallas kernels, local(): pl.pallas_call(kernel, out_shape=(out(TOK, D), out(D // NY, FF), out(D //...  184 us
    unnamed x10, local copies, waits for them, and re-layouts  5.67 us

profile of v2, /device:TPU:1, one launch (start us, length us, event | category | flops | bytes accessed | tf_op | source)
XLA Modules:
  0.0 190.0 jit_solution(17360635225167397501)
XLA Ops:
  0.6 183.7 %shard_map.102 = (bf16[128,2048]{1,0:T(8,128)(2,1)}, bf16[512,768]{1,0:T(8,128)(2,1)}, bf16[512,768]{1,0:T(8,128)(2,1)}, bf16[768,512]{1,0:T(8,128)(2,1)}) custom-call(bf16[128,2048]{1,0:T(8,128)(2,1)} %tok.1, bf16[128,2048]{1,0:T(8,128)(2,1)} %og.1, s32[4,128]{1,0:T(4,128)} %bitcast.14, f32[4,128]{1,0:T(4,128)} %bitcast.15, bf16[512,768]{1,0:T(8,128)(2,1)} %bitcast.11, ...), custom_call_target="tpu_custom_call" | custom-call | tf_op jit(solution)/shard_map/pallas_call | solution.py:558
  184.3 0.0 copy-start.2
  184.3 2.0 %copy.15 = bf16[128,2048]{1,0:T(8,128)(2,1)} copy(bf16[128,2048]{1,0:T(8,128)(2,1)} %get-tuple-element.16) | data formatting | bytes 1048576
  186.3 0.0 copy-done.2
  186.3 0.0 copy-start.1
  186.3 0.9 copy.16
  187.2 0.5 copy-done.1
  187.7 0.0 copy-start
  187.7 0.9 copy.17
  188.6 0.5 copy-done
  189.1 0.9 copy.18
Async XLA Ops:
  184.3 2.0 %copy-start.2 = (bf16[512,768]{1,0:T(8,128)(2,1)S(1)}, bf16[512,768]{1,0:T(8,128)(2,1)}, u32[]{:S(2)}) copy-start(bf16[512,768]{1,0:T(8,128)(2,1)} %get-tuple-element.9) | copy-start | bytes 2359300
  186.3 1.4 copy-start.1
  187.7 1.4 copy-start

commit v3 on v2

--- a/solution.py
+++ b/solution.py
@@ -393,6 +393,7 @@
     first_matmul(0, fg, act)
     z_step(5, 2)
     z_step(6, 2)
+    y_forward(2)
     x_end(2)
     x_end(3)
     first_matmul(1, fg, act)
@@ -401,16 +402,15 @@
     z_step(6, 3)
     y_end(1)
     first_matmul(0, fu, up)
-    y_forward(2)
     gather(5)
     gather(6)
     z_step(7, 2)
     first_matmul(1, fu, up)
-    z_step(7, 3)
     activations()
     x_end(4)
     part(0, 0)
     g_begin(0)
+    z_step(7, 3)
     gather(7)
     x_end(5)
     part(0, 1)

time: 190 us -> 190 us (level)
  no operation moved by 1% of the time
where the time goes in v3:
time: 190 us
  Pallas kernels  183 us (96%)
  local copies, waits for them, and re-layouts  5.67 us (3%)
    pallas_call x1, Pallas kernels, local(): pl.pallas_call(kernel, out_shape=(out(TOK, D), out(D // NY, FF), out(D //...  183 us
    unnamed x10, local copies, waits for them, and re-layouts  5.67 us

profile of v3, /device:TPU:1, one launch (start us, length us, event | category | flops | bytes accessed | tf_op | source)
XLA Modules:
  0.0 189.7 jit_solution(7911860842385136725)
XLA Ops:
  0.6 183.3 %shard_map.102 = (bf16[128,2048]{1,0:T(8,128)(2,1)}, bf16[512,768]{1,0:T(8,128)(2,1)}, bf16[512,768]{1,0:T(8,128)(2,1)}, bf16[768,512]{1,0:T(8,128)(2,1)}) custom-call(bf16[128,2048]{1,0:T(8,128)(2,1)} %tok.1, bf16[128,2048]{1,0:T(8,128)(2,1)} %og.1, s32[4,128]{1,0:T(4,128)} %bitcast.14, f32[4,128]{1,0:T(4,128)} %bitcast.15, bf16[512,768]{1,0:T(8,128)(2,1)} %bitcast.11, ...), custom_call_target="tpu_custom_call" | custom-call | tf_op jit(solution)/shard_map/pallas_call | solution.py:558
  184.0 0.0 copy-start.2
  184.0 2.0 %copy.15 = bf16[128,2048]{1,0:T(8,128)(2,1)} copy(bf16[128,2048]{1,0:T(8,128)(2,1)} %get-tuple-element.16) | data formatting | bytes 1048576
  185.9 0.0 copy-done.2
  185.9 0.0 copy-start.1
  186.0 0.9 copy.16
  186.8 0.5 copy-done.1
  187.4 0.0 copy-start
  187.4 0.9 copy.17
  188.2 0.5 copy-done
  188.8 0.9 copy.18
Async XLA Ops:
  184.0 2.0 %copy-start.2 = (bf16[512,768]{1,0:T(8,128)(2,1)S(1)}, bf16[512,768]{1,0:T(8,128)(2,1)}, u32[]{:S(2)}) copy-start(bf16[512,768]{1,0:T(8,128)(2,1)} %get-tuple-element.9) | copy-start | bytes 2359300
  185.9 1.4 copy-start.1
  187.4 1.4 copy-start
